TPU v7x, 128 devices: a whole 4x4x4 slice. The times are simulated.
128 devices in a mesh: arc: 8 (over x, core), par: 16 (over y, z).
Axes of the slice: x: 4, y: 4, z: 4, core: 2. Of those that a mesh axis runs over, the one named last changes fastest.
Arguments:
- observations: float32 [2048, 65536], P('arc', 'par'), may hold values from -18 to 18
- arc_mask: int32 [16, 512], P('arc', 'par'), may hold values 0 or 1
- panel_owner: int32 [2], replicated, may hold values from 0 to 255, as said below
Outputs:
- info_rows: float32 [512, 65536], P('arc', 'par')
Inputs may be any that keep to these rules, and one draw needn't show every extreme that they name: `panel_owner`: two different panel indices below 256; one of the two is always the last panel.
All inputs are finite; a program needn't handle non-finite values. No bound on the sum of `arc_mask` on one device may be relied on, other than what follows from the above.
Results may differ from a plain program's by a relative error of at most 0.002.
Values sent between devices are 32-bit elements; how exact they have to be, the bound alone decides.
A program may use at most 64 MiB of HBM per device.

v0:
```python
import math
import jax
import jax.numpy as jnp
from jax import lax
from jax.sharding import PartitionSpec as P

PANEL = 256
BLK = 128


def spread(array, axis, root):
    mine = lax.axis_index(axis) == root
    return lax.psum(jnp.where(mine, array, jnp.zeros_like(array)), axis)


def matmul_high(left, right):
    return jnp.dot(left, right, precision=lax.Precision.HIGHEST, preferred_element_type=jnp.float32)


def inner_high(left, right):
    return lax.dot_general(
        left,
        right,
        (((0,), (0,)), ((), ())),
        precision=lax.Precision.HIGHEST,
        preferred_element_type=jnp.float32,
    )


def cholesky_loop(gram):
    order = gram.shape[0]
    positions = lax.broadcasted_iota(jnp.int32, (order, 1), 0)

    def one_column(column, lower):
        lower_row = lax.dynamic_slice_in_dim(lower, column, 1, 0)
        gram_col = lax.dynamic_slice_in_dim(gram, column, 1, 1)
        values = gram_col - matmul_high(lower, lower_row.T)
        pivot = lax.dynamic_slice_in_dim(values, column, 1, 0)
        scaled = jnp.where(positions >= column, values / jnp.sqrt(pivot), 0.0)
        return lax.dynamic_update_slice_in_dim(lower, scaled, column, 1)

    return lax.fori_loop(0, order, one_column, jnp.zeros_like(gram))


def lower_inverse(lower):
    order = lower.shape[0]
    columns = lax.broadcasted_iota(jnp.int32, (1, order), 1)

    def one_row(index, inverse):
        lower_row = lax.dynamic_slice_in_dim(lower, index, 1, 0)
        diag_entry = lax.dynamic_slice_in_dim(lower_row, index, 1, 1)
        unit_row = jnp.where(columns == index, 1.0, 0.0).astype(jnp.float32)
        new_row = (unit_row - matmul_high(lower_row, inverse)) / diag_entry
        return lax.dynamic_update_slice_in_dim(inverse, new_row, index, 0)

    return lax.fori_loop(0, order, one_row, jnp.zeros_like(lower))


def share_panel(design, panel_index):
    col_count = design.shape[1]
    col_start = panel_index * PANEL
    owner_root = col_start // col_count
    offset = col_start - owner_root * col_count
    local_cols = lax.dynamic_slice_in_dim(design, offset, PANEL, 1)
    return spread(local_cols, "par", owner_root)


def own_rows(stacked):
    arc_count = lax.axis_size("arc")
    row_share = stacked.shape[0] // arc_count
    row_start = lax.axis_index("arc") * row_share
    return lax.dynamic_slice_in_dim(stacked, row_start, row_share, 0)


def shards(observations, arc_mask, panel_owner):
    row_count, col_count = observations.shape
    row_blocks, col_blocks = arc_mask.shape
    total_rows = row_count * lax.axis_size("arc")
    shaped = observations.reshape(row_blocks, BLK, col_blocks, BLK)
    masked = shaped * arc_mask.astype(jnp.float32)[:, None, :, None]
    design = masked.reshape(row_count, col_count) / math.sqrt(total_rows)
    rows_out = []
    for panel_turn in range(2):
        panel_cols = share_panel(design, panel_owner[panel_turn])
        gram_block, cross_sums = lax.psum(
            (inner_high(panel_cols, panel_cols), inner_high(panel_cols, design)), "arc"
        )
        inverse = lower_inverse(cholesky_loop(gram_block))
        factor = matmul_high(inverse, cross_sums)
        rows_out.append(factor)
        if panel_turn == 0:
            coefficients = matmul_high(inverse.T, factor)
            design = design - matmul_high(panel_cols, coefficients)
    return own_rows(jnp.concatenate(rows_out, 0))


def solution(mesh):
    return jax.shard_map(
        shards,
        mesh=mesh,
        in_specs=(P("arc", "par"), P("arc", "par"), P()),
        out_specs=P("arc", "par"),
        check_vma=False,
    )
```

profile of v0, /device:TPU:0, one launch (start us, length us, event | category | flops | bytes accessed | tf_op | source)
XLA Modules:
  0.0 2377.6 jit_solution(8174050808208383253)
XLA Ops:
  6.5 1.4 fusion.28
  9.9 1.6 copy-done.5
  11.5 4.1 fusion.24
  15.6 2.0 copy-done
  18.3 87.0 %all-reduce.7.cloned.1.call-done = f32[256,256]{1,0:T(8,128)} async-done(((f32[256,256]{1,0:T(8,128)}), f32[256,256]{1,0:T(8,128)}) %all-reduce.7.cloned.1.call-update) | async-done | bytes 262160 | tf_op jit(solution)/shard_map/psum | solution.py:13
  105.4 8.0 fusion.30
  113.4 1.3 fusion.29
  115.6 72.0 %all-reduce.13.cloned.1.call-done = (f32[256,256]{1,0:T(8,128)}, f32[256,4096]{1,0:T(8,128)}) async-done(((f32[256,256]{1,0:T(8,128)}, f32[256,4096]{1,0:T(8,128)}), (f32[256,256]{1,0:T(8,128)}, f32[256,4096]{1,0:T(8,128)})) %all-reduce.13.cloned.1.call-update) | async-done | bytes 4456464 | tf_op jit(solution)/shard_map/psum | solution.py:85
  187.5 1.1 copy.11
  188.7 602.1 %while.62 = (s32[]{:T(128)}, f32[256,256]{1,0:T(8,128)S(1)}, f32[256,256]{0,1:T(8,128)S(1)}, s32[]{:T(128)}, s32[]{:T(128)}) while((s32[]{:T(128)}, f32[256,256]{1,0:T(8,128)S(1)}, f32[256,256]{0,1:T(8,128)S(1)}, s32[]{:T(128)}, s32[]{:T(128)}) %tuple.138), condition=%wide.region_3.4_spmd.clone, body=%wide.region_2.3_spmd.clone.sunk | while | flops 787458 | bytes 272469 | solution.py:42
  790.8 393.8 %while.63 = (s32[]{:T(128)}, f32[256,256]{1,0:T(8,128)S(1)}, f32[256,256]{1,0:T(8,128)S(1)}, s32[]{:T(128)}, s32[]{:T(128)}, /*index=5*/s32[]{:T(128)}) while((s32[]{:T(128)}, f32[256,256]{1,0:T(8,128)S(1)}, f32[256,256]{1,0:T(8,128)S(1)}, s32[]{:T(128)}, s32[]{:T(128)}, /*index=5*/s32[]{:T(128)}) %tuple.141), condition=%wide.region_5.6_spmd.clone, body=%wide.region_4.5_spmd.clone.sunk | while | flops 787459 | bytes 270449 | solution.py:56
  1184.6 5.4 fusion.31
  1190.0 3.8 fusion.32
  1193.9 3.8 convolution_subtract_fusion
  1197.7 2.0 copy-done.4
  1200.6 84.5 %all-reduce.9.cloned.1.call-done = f32[256,256]{1,0:T(8,128)} async-done(((f32[256,256]{1,0:T(8,128)}), f32[256,256]{1,0:T(8,128)}) %all-reduce.9.cloned.1.call-update) | async-done | bytes 262160 | tf_op jit(solution)/shard_map/psum | solution.py:13
  1285.1 8.0 fusion.34
  1293.1 1.3 fusion.33
  1294.5 72.8 %all-reduce.11.cloned.1.call-done = (f32[256,256]{1,0:T(8,128)}, f32[256,4096]{1,0:T(8,128)}) async-done(((f32[256,256]{1,0:T(8,128)}, f32[256,4096]{1,0:T(8,128)}), (f32[256,256]{1,0:T(8,128)}, f32[256,4096]{1,0:T(8,128)})) %all-reduce.11.cloned.1.call-update) | async-done | bytes 4456464 | tf_op jit(solution)/shard_map/psum | solution.py:85
  1367.3 1.1 copy.12
  1368.4 602.1 %while.64 = (s32[]{:T(128)}, f32[256,256]{1,0:T(8,128)S(1)}, f32[256,256]{0,1:T(8,128)S(1)}, s32[]{:T(128)}, s32[]{:T(128)}) while((s32[]{:T(128)}, f32[256,256]{1,0:T(8,128)S(1)}, f32[256,256]{0,1:T(8,128)S(1)}, s32[]{:T(128)}, s32[]{:T(128)}) %tuple.144), condition=%wide.region_10.11_spmd.clone, body=%wide.region_9.10_spmd.clone.sunk | while | flops 787458 | bytes 272469 | solution.py:42
  1970.5 393.8 %while.65 = (s32[]{:T(128)}, f32[256,256]{1,0:T(8,128)S(1)}, f32[256,256]{1,0:T(8,128)S(1)}, s32[]{:T(128)}, s32[]{:T(128)}, /*index=5*/s32[]{:T(128)}) while((s32[]{:T(128)}, f32[256,256]{1,0:T(8,128)S(1)}, f32[256,256]{1,0:T(8,128)S(1)}, s32[]{:T(128)}, s32[]{:T(128)}, /*index=5*/s32[]{:T(128)}) %tuple.147), condition=%wide.region_12.13_spmd.clone, body=%wide.region_11.12_spmd.clone.sunk | while | flops 787459 | bytes 270449 | solution.py:56
  2364.4 5.6 fusion.35
  2370.0 1.1 fusion.25
  (5149 shorter events, 1960.7 us)
Async XLA Ops:
  6.5 98.8 %all-reduce.7.cloned.1.call-start = ((), (), s32[]{:S(2)}) async-start(), calls=%async_computation | async-start | bytes 524288 | tf_op jit(solution)/shard_map/psum | solution.py:13
  9.3 2.2 copy-start.5
  15.6 2.0 copy-start
  18.3 169.3 %all-reduce.13.cloned.1.call-start = ((), (), s32[]{:S(2)}) async-start(), calls=%async_computation.3 | async-start | bytes 8912896 | tf_op jit(solution)/shard_map/psum | solution.py:85
  105.3 8.0 copy-start.6
  114.7 1170.4 %all-reduce.9.cloned.1.call-start = ((), (), s32[]{:S(2)}) async-start(), calls=%async_computation.1 | async-start | bytes 524288 | tf_op jit(solution)/shard_map/psum | solution.py:13
  1190.0 3.8 copy-start.2
  1190.0 3.8 copy-start.1
  1197.7 2.0 copy-start.4
  1200.4 166.9 %all-reduce.11.cloned.1.call-start = ((), (), s32[]{:S(2)}) async-start(), calls=%async_computation.2 | async-start | bytes 8912896 | tf_op jit(solution)/shard_map/psum | solution.py:85
  1285.1 8.0 copy-start.7
  2364.4 5.6 copy-start.3
Sparse Core Ops, SparseCore 0:
  18.4 86.9 all-reduce.6
  114.8 72.6 all-reduce.12
  1200.5 84.5 all-reduce.8
  1294.6 72.6 all-reduce.10
where the time goes:
time: 2390 us; the launch traced here: 2380 us
  local copies, waits for them, and re-layouts  1070 us (45%)
  other arithmetic  675 us (28%)
  waiting for transfers between devices  316 us (13%)
  matrix products  270 us (11%)
  loops' own time  34.5 us (1%)
    select_n x512, other arithmetic, one_column(): scaled = jnp.where(positions >= column, values / jnp.sqrt(pivot), 0.0)  333 us
    sqrt x512, local copies, waits for them, and re-layouts, one_column(): scaled = jnp.where(positions >= column, values / jnp.sqrt(pivot), 0.0)  332 us
    div x512, other arithmetic, one_row(): new_row = (unit_row - matmul_high(lower_row, inverse)) / diag_entry  332 us
    dynamic_slice x512, local copies, waits for them, and re-layouts, one_row(): diag_entry = lax.dynamic_slice_in_dim(lower_row, index, 1, 1)  321 us
    dynamic_update_slice x512, local copies, waits for them, and re-layouts, one_column(): return lax.dynamic_update_slice_in_dim(lower, scaled, column, 1)  314 us
    dot_general x1028, matrix products, matmul_high(): jnp.dot(left, right, precision=lax.Precision.HIGHEST, preferred_element_t...  251 us
    psum x2, waiting for transfers between devices, spread(): return lax.psum(jnp.where(mine, array, jnp.zeros_like(array)), axis)  171 us
    psum x2, waiting for transfers between devices, shards(): lax.psum((inner_high(panel_cols, panel_cols), inner_high(panel_cols, desi...  145 us

commit v1 on v0

--- a/solution.py
+++ b/solution.py
@@ -8,9 +8,15 @@
 BLK = 128
 
 
+def gather_and_add(x, axis):
+    blocks = lax.all_gather(x, axis, axis=0, tiled=False)
+    acc = blocks.sum(axis=0)
+    return acc
+
+
 def spread(array, axis, root):
     mine = lax.axis_index(axis) == root
-    return lax.psum(jnp.where(mine, array, jnp.zeros_like(array)), axis)
+    return gather_and_add(jnp.where(mine, array, jnp.zeros_like(array)), axis)
 
 
 def matmul_high(left, right):

time: 2390 us -> 2330 us (0.975)
  waiting for transfers between devices: 316 us -> 252 us
    psum x2 -> x0, waiting for transfers between devices: 171 us -> none  [spread(): return lax.psum(jnp.where(mine, array, jnp.zeros_like(array)), axis)]
    all_gather x0 -> x2, waiting for transfers between devices: none -> 106 us  [gather_and_add(): blocks = lax.all_gather(x, axis, axis=0, tiled=False)]
where the time goes in v1:
time: 2330 us; the launch traced here: 2320 us
  local copies, waits for them, and re-layouts  1070 us (46%)
  other arithmetic  680 us (29%)
  matrix products  270 us (12%)
  waiting for transfers between devices  252 us (11%)
  loops' own time  34.5 us (1%)
    select_n x512, other arithmetic, one_column(): scaled = jnp.where(positions >= column, values / jnp.sqrt(pivot), 0.0)  333 us
    sqrt x512, local copies, waits for them, and re-layouts, one_column(): scaled = jnp.where(positions >= column, values / jnp.sqrt(pivot), 0.0)  332 us
    div x512, other arithmetic, one_row(): new_row = (unit_row - matmul_high(lower_row, inverse)) / diag_entry  332 us
    dynamic_slice x512, local copies, waits for them, and re-layouts, one_row(): diag_entry = lax.dynamic_slice_in_dim(lower_row, index, 1, 1)  321 us
    dynamic_update_slice x512, local copies, waits for them, and re-layouts, one_column(): return lax.dynamic_update_slice_in_dim(lower, scaled, column, 1)  314 us
    dot_general x1028, matrix products, matmul_high(): jnp.dot(left, right, precision=lax.Precision.HIGHEST, preferred_element_t...  251 us
    psum x2, waiting for transfers between devices, shards(): lax.psum((inner_high(panel_cols, panel_cols), inner_high(panel_cols, desi...  146 us
    all_gather x2, waiting for transfers between devices, gather_and_add(): blocks = lax.all_gather(x, axis, axis=0, tiled=False)  106 us

profile of v1, /device:TPU:0, one launch (start us, length us, event | category | flops | bytes accessed | tf_op | source)
XLA Modules:
  0.0 2317.9 jit_solution(3139214873398760220)
XLA Ops:
  6.5 1.3 fusion.28
  9.8 1.6 copy-done.5
  11.4 4.1 fusion.24
  15.5 1.9 copy-done
  18.3 54.2 %all-gather.5.cloned.1.call-done = f32[4096,256]{1,0:T(8,128)} async-done(((f32[256,256]{1,0:T(8,128)}), f32[4096,256]{1,0:T(8,128)}) %all-gather.5.cloned.1.call-update) | async-done | bytes 4194320 | tf_op jit(solution)/shard_map/all_gather | solution.py:12
  72.5 2.5 reduce_sum.18
  75.0 8.2 fusion.30
  83.1 1.3 fusion.29
  85.3 72.4 %all-reduce.7.cloned.1.call-done = (f32[256,256]{1,0:T(8,128)}, f32[256,4096]{1,0:T(8,128)}) async-done(((f32[256,256]{1,0:T(8,128)}, f32[256,4096]{1,0:T(8,128)}), (f32[256,256]{1,0:T(8,128)}, f32[256,4096]{1,0:T(8,128)})) %all-reduce.7.cloned.1.call-update) | async-done | bytes 4456464 | tf_op jit(solution)/shard_map/psum | solution.py:91
  158.8 602.1 %while.62 = (s32[]{:T(128)}, f32[256,256]{1,0:T(8,128)S(1)}, f32[256,256]{0,1:T(8,128)S(1)}, s32[]{:T(128)}, s32[]{:T(128)}) while((s32[]{:T(128)}, f32[256,256]{1,0:T(8,128)S(1)}, f32[256,256]{0,1:T(8,128)S(1)}, s32[]{:T(128)}, s32[]{:T(128)}) %tuple.138), condition=%wide.region_3.4_spmd.clone, body=%wide.region_2.3_spmd.clone.sunk | while | flops 787458 | bytes 272469 | solution.py:48
  760.9 393.8 %while.63 = (s32[]{:T(128)}, f32[256,256]{1,0:T(8,128)S(1)}, f32[256,256]{1,0:T(8,128)S(1)}, s32[]{:T(128)}, s32[]{:T(128)}, /*index=5*/s32[]{:T(128)}) while((s32[]{:T(128)}, f32[256,256]{1,0:T(8,128)S(1)}, f32[256,256]{1,0:T(8,128)S(1)}, s32[]{:T(128)}, s32[]{:T(128)}, /*index=5*/s32[]{:T(128)}) %tuple.141), condition=%wide.region_5.6_spmd.clone, body=%wide.region_4.5_spmd.clone.sunk | while | flops 787459 | bytes 270449 | solution.py:62
  1154.7 5.4 fusion.31
  1160.1 3.8 fusion.32
  1164.0 3.8 convolution_subtract_fusion
  1167.8 1.9 copy-done.4
  1170.7 51.7 %all-gather.7.cloned.1.call-done = f32[4096,256]{1,0:T(8,128)} async-done(((f32[256,256]{1,0:T(8,128)}), f32[4096,256]{1,0:T(8,128)}) %all-gather.7.cloned.1.call-update) | async-done | bytes 4194320 | tf_op jit(solution)/shard_map/all_gather | solution.py:12
  1222.4 2.5 reduce_sum.19
  1224.9 8.2 fusion.34
  1233.1 1.3 fusion.33
  1234.4 73.2 %all-reduce.5.cloned.1.call-done = (f32[256,256]{1,0:T(8,128)}, f32[256,4096]{1,0:T(8,128)}) async-done(((f32[256,256]{1,0:T(8,128)}, f32[256,4096]{1,0:T(8,128)}), (f32[256,256]{1,0:T(8,128)}, f32[256,4096]{1,0:T(8,128)})) %all-reduce.5.cloned.1.call-update) | async-done | bytes 4456464 | tf_op jit(solution)/shard_map/psum | solution.py:91
  1308.7 602.1 %while.64 = (s32[]{:T(128)}, f32[256,256]{1,0:T(8,128)S(1)}, f32[256,256]{0,1:T(8,128)S(1)}, s32[]{:T(128)}, s32[]{:T(128)}) while((s32[]{:T(128)}, f32[256,256]{1,0:T(8,128)S(1)}, f32[256,256]{0,1:T(8,128)S(1)}, s32[]{:T(128)}, s32[]{:T(128)}) %tuple.144), condition=%wide.region_10.11_spmd.clone, body=%wide.region_9.10_spmd.clone.sunk | while | flops 787458 | bytes 272469 | solution.py:48
  1910.8 393.8 %while.65 = (s32[]{:T(128)}, f32[256,256]{1,0:T(8,128)S(1)}, f32[256,256]{1,0:T(8,128)S(1)}, s32[]{:T(128)}, s32[]{:T(128)}, /*index=5*/s32[]{:T(128)}) while((s32[]{:T(128)}, f32[256,256]{1,0:T(8,128)S(1)}, f32[256,256]{1,0:T(8,128)S(1)}, s32[]{:T(128)}, s32[]{:T(128)}, /*index=5*/s32[]{:T(128)}) %tuple.147), condition=%wide.region_12.13_spmd.clone, body=%wide.region_11.12_spmd.clone.sunk | while | flops 787459 | bytes 270449 | solution.py:62
  2304.7 5.6 fusion.35
  2310.3 1.1 fusion.25
  (5147 shorter events, 1962.9 us)
Async XLA Ops:
  6.5 66.0 %all-gather.5.cloned.1.call-start = ((), (), s32[]{:S(2)}) async-start(), calls=%async_computation | async-start | bytes 4456448 | tf_op jit(solution)/shard_map/all_gather | solution.py:12
  9.2 2.2 copy-start.5
  15.5 2.0 copy-start
  18.2 139.4 %all-reduce.7.cloned.1.call-start = ((), (), s32[]{:S(2)}) async-start(), calls=%async_computation.3 | async-start | bytes 8912896 | tf_op jit(solution)/shard_map/psum | solution.py:91
  84.5 1138.0 %all-gather.7.cloned.1.call-start = ((), (), s32[]{:S(2)}) async-start(), calls=%async_computation.1 | async-start | bytes 4456448 | tf_op jit(solution)/shard_map/all_gather | solution.py:12
  1160.1 3.8 copy-start.2
  1160.1 3.8 copy-start.1
  1167.8 2.0 copy-start.4
  1170.5 137.1 %all-reduce.5.cloned.1.call-start = ((), (), s32[]{:S(2)}) async-start(), calls=%async_computation.2 | async-start | bytes 8912896 | tf_op jit(solution)/shard_map/psum | solution.py:91
  2304.7 5.6 copy-start.3
Sparse Core Ops, SparseCore 0:
  18.3 54.1 all-gather.4
  84.6 73.0 all-reduce.6
  1170.6 51.8 all-gather.6
  1234.5 73.0 all-reduce.4
